TPU v7x, 32 devices: a whole 2x2x4 slice. The times are simulated.
32 devices in a mesh: pipe: 4 (over x, core), dp: 8 (over z, y).
Axes of the slice: x: 2, y: 2, z: 4, core: 2. Of those that a mesh axis runs over, the one named last changes fastest.
Arguments:
- token_ids: int32 [96, 126], P('dp'), may hold values from 0 to 1023
- segment_ids: int32 [96, 126], P('dp'), may hold values from 0 to 3, never falling along the last dimension, each value on 1 to 63 neighbouring positions
- target_ids: int32 [96, 126], P('dp'), may hold values from 0 to 1023
- embed_table: bfloat16 [1024, 512], replicated, may hold values from -6 to 6
- qkv_weight: bfloat16 [4, 512, 1536], P('pipe'), may hold values from -0.25 to 0.25
- qv_bias: float32 [4, 2, 512], P('pipe'), may hold values from -1.75 to 1.75
- out_weight: bfloat16 [4, 512, 512], P('pipe'), may hold values from -1 to 1
- out_biases: float32 [4, 2, 512], P('pipe'), may hold values from -1.75 to 1.75
- ff_in: bfloat16 [4, 512, 2048], P('pipe'), may hold values from -0.25 to 0.25
- ff_in_bias: float32 [4, 2048], P('pipe'), may hold values from -1.75 to 1.75
- ff_out: bfloat16 [4, 2048, 512], P('pipe'), may hold values from -0.125 to 0.125
- norm_gains: float32 [4, 2, 512], P('pipe'), may hold values from 0.5 to 1.5
- norm_biases: float32 [4, 2, 512], P('pipe'), may hold values from -1.75 to 1.75
- final_gain: float32 [512], replicated, may hold values from 0.5 to 1.5
- final_bias: float32 [512], replicated, may hold values from -1.75 to 1.75
- head_weight: bfloat16 [1024, 512], replicated, may hold values from -0.5 to 0.5
Outputs:
- embed_grad: float32 [1024, 512], P(('pipe', 'dp'))
- qkv_grad: float32 [4, 512, 1536], P('pipe', 'dp')
- qv_bias_grad: float32 [4, 2, 512], P('pipe', None, 'dp')
- out_weight_grad: float32 [4, 512, 512], P('pipe', 'dp')
- out_biases_grad: float32 [4, 2, 512], P('pipe', None, 'dp')
- ff_in_grad: float32 [4, 512, 2048], P('pipe', 'dp')
- ff_in_bias_grad: float32 [4, 2048], P('pipe', 'dp')
- ff_out_grad: float32 [4, 2048, 512], P('pipe', 'dp')
- norm_gains_grad: float32 [4, 2, 512], P('pipe', None, 'dp')
- norm_biases_grad: float32 [4, 2, 512], P('pipe', None, 'dp')
- final_gain_grad: float32 [512], replicated
- final_bias_grad: float32 [512], replicated
- head_grad: float32 [1024, 512], P(('pipe', 'dp'))
Inputs may be any that keep to these rules, and one draw needn't show every extreme that they name: `segment_ids`: along a row segment numbers never fall; a fragment has at most 63 tokens.
All inputs are finite; a program needn't handle non-finite values.
Results may differ from a plain program's by a relative error of at most 0.0055.
Values may be sent and summed in bfloat16 or wider, within the bound.
A program may use at most 256 MiB of HBM per device.

v0:
```python
import functools

import jax
import jax.numpy as jnp
from jax import lax
from jax.experimental import pallas as pl
from jax.experimental.pallas import tpu as pltpu
from jax.sharding import PartitionSpec as P

HEADS = 8
FRAME = 6
ROW = 128
GROUP = 2
MASKED = -1e30
GELU_A = 0.7978845608
GELU_B = 0.044715
MESH = pl.DeviceIdType.MESH
F32 = jnp.float32
BF16 = jnp.bfloat16

VEC_ROWS = 16
V_QUERY, V_VALUE, V_BRANCH, V_RESULT, V_GAIN1, V_GAIN2, V_SHIFT1, V_SHIFT2 = range(8)
V_HIDDEN = 8
V_FINAL_GAIN, V_FINAL_BIAS = 12, 13


def dot(a, b):
    return lax.dot_general(a, b, (((1,), (0,)), ((), ())), preferred_element_type=F32)


def dot_nt(a, b):
    return lax.dot_general(a, b, (((1,), (1,)), ((), ())), preferred_element_type=F32)


def dot_tn(a, b):
    return lax.dot_general(a, b, (((0,), (0,)), ((), ())), preferred_element_type=F32)


def normalise(values):
    centre = jnp.mean(values, axis=-1, keepdims=True)
    centered = values - centre
    spread = jnp.mean(centered * centered, axis=-1, keepdims=True)
    scale = lax.rsqrt(spread + 1e-05)
    return centered * scale, scale


def norm_backward(grad, normal, scale, gain):
    grad_n = grad * gain
    mean_grad = jnp.mean(grad_n, axis=-1, keepdims=True)
    mean_proj = jnp.mean(grad_n * normal, axis=-1, keepdims=True)
    return scale * (grad_n - mean_grad - normal * mean_proj)


def column_sum(values):
    return jnp.sum(values, axis=0, keepdims=True)


def stack_pair(pair, low_lanes):
    zero = jnp.zeros_like(pair)
    return jnp.concatenate(
        [jnp.where(low_lanes, pair, zero), jnp.where(low_lanes, zero, pair)], axis=0
    )


def join_pair(stacked, low_lanes):
    half = stacked.shape[0] // 2
    return jnp.where(low_lanes, stacked[:half], stacked[half:])


def pipeline_kernel(
    stages,
    micros,
    token_ids,
    segment_ids,
    target_ids,
    embed,
    qkv_w,
    qv_b,
    out_w,
    out_b,
    in_w,
    in_b,
    down_w,
    gains,
    shifts,
    fin_gain,
    fin_bias,
    head_w,
    normed_o,
    mixed_o,
    normed2_o,
    active_o,
    gres_o,
    ghid_o,
    gbr_o,
    gproj_o,
    xl_o,
    xr_o,
    vec,
    instream,
    outb,
    gin,
    gs,
    normed,
    proj,
    probs,
    mixed,
    middle,
    normed2,
    active,
    slope,
    lo,
    go,
    gmid,
    s_gres,
    s_ghid,
    s_gbr,
    s_gproj,
    s_xl,
    ids,
    frames,
    fsend,
    frecv,
    bsend,
    brecv,
    osem,
):
    stage = lax.axis_index("pipe")
    tokens, width = instream.shape[1], instream.shape[2]
    hidden_n = in_b.shape[1]
    vocab = head_w.shape[0]
    pairs = width // ROW
    chunk = 512
    is_first = stage == 0
    is_last = stage == stages - 1
    up = jnp.minimum(stage + 1, stages - 1)
    down = jnp.maximum(stage - 1, 0)

    barrier = pltpu.get_barrier_semaphore()

    @pl.when(jnp.logical_not(is_first))
    def _():
        pl.semaphore_signal(barrier, inc=1, device_id={"pipe": down}, device_id_type=MESH)

    @pl.when(jnp.logical_not(is_last))
    def _():
        pl.semaphore_signal(barrier, inc=1, device_id={"pipe": up}, device_id_type=MESH)

    pl.semaphore_wait(barrier, jnp.where(is_first | is_last, 1, 2))
    vec[...] = jnp.zeros_like(vec)
    rows_n, seq = token_ids.shape
    for index, member in enumerate((token_ids, segment_ids, target_ids)):
        ids[index] = jnp.full(ids.shape[1:], 4.0 if index == 1 else -1.0, F32)
        ids[index, 0:rows_n, 0:seq] = member[...].astype(F32)
    at_query = lax.broadcasted_iota(jnp.int32, (ROW, ROW), 1)
    at_key = lax.broadcasted_iota(jnp.int32, (ROW, ROW), 0)
    frames[...] = jnp.where(at_key < ((at_query * 43) // 256) * FRAME + FRAME, 1.0, 0.0)

    def column(index, row):
        values = jnp.broadcast_to(ids[index, pl.ds(row, 1), :], (8, ROW))
        return values.T[:, 0:1]

    def hot_rows(index, m):
        parts = [column(index, m * GROUP + r) for r in range(GROUP)]
        values = jnp.concatenate(parts, axis=0)
        places = lax.broadcasted_iota(jnp.int32, (tokens, vocab), 1).astype(F32)
        return values, jnp.where(values == places, 1.0, 0.0)

    def forward_copy(m):
        return pltpu.make_async_remote_copy(
            src_ref=outb.at[m],
            dst_ref=instream.at[m],
            send_sem=fsend.at[m],
            recv_sem=frecv.at[m],
            device_id={"pipe": up},
            device_id_type=MESH,
        )

    def backward_copy(m):
        return pltpu.make_async_remote_copy(
            src_ref=gs.at[m],
            dst_ref=gin.at[m],
            send_sem=bsend.at[m],
            recv_sem=brecv.at[m],
            device_id={"pipe": down},
            device_id_type=MESH,
        )

    def save(index, src, dst, m):
        return pltpu.make_async_copy(src, dst.at[m], osem.at[index, m])

    def saves_forward(m):
        return [
            save(0, normed.at[m], normed_o, m),
            save(1, mixed.at[m], mixed_o, m),
            save(2, normed2.at[m], normed2_o, m),
            save(3, active.at[m], active_o, m),
        ]

    def saves_backward(m):
        slot = lax.rem(m, 2)
        return [
            save(4, s_gres.at[slot], gres_o, m),
            save(5, s_ghid.at[slot], ghid_o, m),
            save(6, s_gbr.at[slot], gbr_o, m),
            save(7, s_gproj.at[slot], gproj_o, m),
        ]

    def save_xl(m):
        return save(8, s_xl.at[lax.rem(m, 2)], xl_o, m)

    def put_xl(m, value):
        @pl.when(m >= 2)
        def _():
            save_xl(m - 2).wait()

        s_xl[lax.rem(m, 2)] = value
        save_xl(m).start()

    lane_low = lax.broadcasted_iota(jnp.int32, (ROW, ROW), 1) < ROW // 2

    def forward(m):
        @pl.when(is_first)
        def _():
            hot = hot_rows(0, m)[1].astype(BF16)
            instream[m] = dot(hot, embed[...]).astype(BF16)

        @pl.when(jnp.logical_not(is_first))
        def _():
            forward_copy(m).wait_recv()

        normal, _ = normalise(instream[m].astype(F32))
        normed[m] = (normal * gains[0:1, :] + shifts[0:1, :]).astype(BF16)
        low = normed[m]
        queries = dot(low, qkv_w[:, 0:width]) + qv_b[0:1, :]
        proj[m, :, 0:width] = (queries * (ROW // 2) ** -0.5).astype(BF16)
        proj[m, :, width : 2 * width] = dot(low, qkv_w[:, width : 2 * width]).astype(BF16)
        proj[m, :, 2 * width : 3 * width] = (
            dot(low, qkv_w[:, 2 * width : 3 * width]) + qv_b[1:2, :]
        ).astype(BF16)
        masks, scores = [], []
        for r in range(GROUP):
            rows = slice(r * ROW, (r + 1) * ROW)
            kinds = lax.broadcasted_iota(jnp.int32, (16, ROW), 0).astype(F32)
            member = jnp.where(ids[1, pl.ds(m * GROUP + r, 1), :] == kinds, 1.0, 0.0).astype(BF16)
            mask = jnp.where(dot_tn(member, member) * frames[...] > 0.5, 0.0, MASKED)
            masks.append(jnp.concatenate([mask, mask], axis=1))
            for p in range(pairs):
                q = stack_pair(proj[m, rows, p * ROW : (p + 1) * ROW], lane_low)
                k = proj[m, rows, width + p * ROW : width + (p + 1) * ROW]
                scores.append(dot_nt(k, q))

        def mix(unit):
            r, p = unit // pairs, unit % pairs
            rows = slice(r * ROW, (r + 1) * ROW)
            v = proj[m, rows, 2 * width + p * ROW : 2 * width + (p + 1) * ROW]
            both = dot_tn(probs[m, unit], v)
            mixed[m, rows, p * ROW : (p + 1) * ROW] = join_pair(both, lane_low).astype(BF16)

        for unit in range(GROUP * pairs):
            masked = scores[unit] + masks[unit // pairs]
            expo = jnp.exp(masked - jnp.max(masked, axis=0, keepdims=True))
            total = jnp.sum(expo, axis=0, keepdims=True)
            probs[m, unit] = (expo * (1.0 / total)).astype(BF16)
            if unit:
                mix(unit - 1)
        mix(GROUP * pairs - 1)
        mid = instream[m].astype(F32) + (dot(mixed[m], out_w[...]) + out_b[0:1, :])
        middle[m] = mid
        normal2, _ = normalise(mid)
        normed2[m] = (normal2 * gains[1:2, :] + shifts[1:2, :]).astype(BF16)
        low2 = normed2[m]
        parts = hidden_n // chunk

        def spread(c):
            return dot(low2, in_w[:, c * chunk : (c + 1) * chunk])

        total, ahead = None, spread(0)
        for c in range(parts):
            cols = slice(c * chunk, (c + 1) * chunk)
            hid = ahead + in_b[0:1, cols]
            if c + 1 < parts:
                ahead = spread(c + 1)
            square = hid * hid
            tan = jnp.tanh(hid * (GELU_A + (GELU_A * GELU_B) * square))
            half = 0.5 + 0.5 * tan
            act = (hid * half).astype(BF16)
            active[m, :, cols] = act
            rise = (1.0 - tan * tan) * (0.5 * GELU_A + (1.5 * GELU_A * GELU_B) * square)
            slope[m, :, cols] = (half + hid * rise).astype(BF16)
            term = dot(act, down_w[cols, :])
            total = term if total is None else total + term
        for copy in saves_forward(m):
            copy.start()
        lo[...] = middle[m] + (total + out_b[1:2, :])

        @pl.when(jnp.logical_not(is_last))
        def _():
            outb[m] = lo[...].astype(BF16)
            forward_copy(m).start()

    def head(m):
        normal, scale = normalise(lo[...])
        outb[m] = (normal * fin_gain[...] + fin_bias[...]).astype(BF16)
        save(9, outb.at[m], xr_o, m).start()
        logits = dot_nt(outb[m], head_w[...])
        top = jnp.max(logits, axis=-1, keepdims=True)
        expo = jnp.exp(logits - top)
        total = jnp.sum(expo, axis=-1, keepdims=True)
        target, hot = hot_rows(2, m)
        grad_logits = jnp.where(target >= 0.0, expo * (1.0 / total) - hot, 0.0).astype(BF16)
        put_xl(m, grad_logits)
        grad_final = dot(grad_logits, head_w[...])
        vec[V_FINAL_GAIN : V_FINAL_GAIN + 1, :] += column_sum(grad_final * normal)
        vec[V_FINAL_BIAS : V_FINAL_BIAS + 1, :] += column_sum(grad_final)
        go[...] = norm_backward(grad_final, normal, scale, fin_gain[...])

    def backward(m):
        slot = lax.rem(m, 2)

        @pl.when(m >= 2)
        def _():
            for copy in saves_backward(m - 2):
                copy.wait()

        @pl.when(jnp.logical_not(is_last))
        def _():
            backward_copy(m).wait_recv()
            go[...] = gin[m].astype(F32)

        s_gres[slot] = go[...].astype(BF16)
        gres = s_gres[slot]
        parts = hidden_n // chunk

        def spread(c):
            return dot_nt(gres, down_w[c * chunk : (c + 1) * chunk, :])

        total, ahead = None, spread(0)
        for c in range(parts):
            cols = slice(c * chunk, (c + 1) * chunk)
            gact = ahead
            if c + 1 < parts:
                ahead = spread(c + 1)
            ghid = (gact * slope[m, :, cols].astype(F32)).astype(BF16)
            s_ghid[slot, :, cols] = ghid
            term = dot_nt(ghid, in_w[:, cols])
            total = term if total is None else total + term
        normal2, scale2 = normalise(middle[m])
        vec[V_GAIN2 : V_GAIN2 + 1, :] += column_sum(total * normal2)
        vec[V_SHIFT2 : V_SHIFT2 + 1, :] += column_sum(total)
        gmid[...] = go[...] + norm_backward(total, normal2, scale2, gains[1:2, :])
        s_gbr[slot] = gmid[...].astype(BF16)
        gbr = s_gbr[slot]
        gmix = dot_nt(gbr, out_w[...]).astype(BF16)
        grads = []
        for r in range(GROUP):
            rows = slice(r * ROW, (r + 1) * ROW)
            for p in range(pairs):
                gm = stack_pair(gmix[rows, p * ROW : (p + 1) * ROW], lane_low)
                vlanes = slice(2 * width + p * ROW, 2 * width + (p + 1) * ROW)
                grads.append(dot_nt(proj[m, rows, vlanes], gm))
                s_gproj[slot, rows, vlanes] = dot(probs[m, r * pairs + p], gm).astype(BF16)

        def pull(unit, gsc):
            r, p = unit // pairs, unit % pairs
            rows = slice(r * ROW, (r + 1) * ROW)
            lanes = slice(p * ROW, (p + 1) * ROW)
            klanes = slice(width + p * ROW, width + (p + 1) * ROW)
            q = stack_pair(proj[m, rows, lanes], lane_low)
            s_gproj[slot, rows, klanes] = dot(gsc, q).astype(BF16)
            gq = join_pair(dot_tn(gsc, proj[m, rows, klanes]), lane_low) * (ROW // 2) ** -0.5
            s_gproj[slot, rows, lanes] = gq.astype(BF16)

        waiting = None
        for unit in range(GROUP * pairs):
            weights = probs[m, unit].astype(F32)
            inner = jnp.sum(weights * grads[unit], axis=0, keepdims=True)
            gsc = (weights * (grads[unit] - inner)).astype(BF16)
            if waiting is not None:
                pull(unit - 1, waiting)
            waiting = gsc
        pull(GROUP * pairs - 1, waiting)
        for copy in saves_backward(m):
            copy.start()
        gproj = s_gproj[slot]
        gnormed = dot_nt(gproj, qkv_w[...])
        normal, scale = normalise(instream[m].astype(F32))
        vec[V_GAIN1 : V_GAIN1 + 1, :] += column_sum(gnormed * normal)
        vec[V_SHIFT1 : V_SHIFT1 + 1, :] += column_sum(gnormed)
        gs[m] = (gmid[...] + norm_backward(gnormed, normal, scale, gains[0:1, :])).astype(BF16)

        @pl.when(is_first)
        def _():
            save(9, gs.at[m], xr_o, m).start()

        @pl.when(jnp.logical_not(is_first))
        def _():
            backward_copy(m).start()

    def tick(t, carry):
        m_forward = t - stage
        m_backward = t - (2 * (stages - 1) - stage)

        @pl.when((m_forward >= 0) & (m_forward < micros))
        def _():
            forward(m_forward)

        @pl.when((m_backward >= 0) & (m_backward < micros))
        def _():
            @pl.when(is_last)
            def _():
                head(m_backward)

            backward(m_backward)

        return carry

    lax.fori_loop(0, micros + 2 * (stages - 1), tick, 0)

    for m in range(micros):
        for copy in saves_forward(m):
            copy.wait()

        @pl.when(jnp.logical_not(is_last))
        def _():
            forward_copy(m).wait_send()

        @pl.when(jnp.logical_not(is_first))
        def _():
            backward_copy(m).wait_send()

        @pl.when(is_first)
        def _():
            save(9, gs.at[m], xr_o, m).wait()

        @pl.when(is_last)
        def _():
            save(9, outb.at[m], xr_o, m).wait()

    for m in range(max(0, micros - 2), micros):
        for copy in saves_backward(m):
            copy.wait()

        @pl.when(is_last)
        def _():
            save_xl(m).wait()


def run_pipeline(stages, token_ids, segment_ids, target_ids, params):
    embed, in_w, head_w = params[0], params[5], params[12]
    width = embed.shape[1]
    vocab = head_w.shape[0]
    hid = in_w.shape[1]
    tokens = GROUP * ROW
    micros = token_ids.shape[0] // GROUP
    pairs = width // ROW
    vmem = pl.BlockSpec(memory_space=pltpu.VMEM)
    hbm = pl.BlockSpec(memory_space=pl.ANY)

    def kept(columns):
        return jax.ShapeDtypeStruct((micros, tokens, columns), BF16)

    def scratch(lead, columns, kind=BF16):
        return pltpu.VMEM((lead, tokens, columns), kind)

    out_shape = [
        kept(width),
        kept(width),
        kept(width),
        kept(hid),
        kept(width),
        kept(hid),
        kept(width),
        kept(3 * width),
        kept(vocab),
        kept(width),
        jax.ShapeDtypeStruct((VEC_ROWS, width), F32),
    ]
    return pl.pallas_call(
        functools.partial(pipeline_kernel, stages, micros),
        out_shape=out_shape,
        in_specs=[vmem] * 16,
        out_specs=[hbm] * 10 + [vmem],
        scratch_shapes=[
            scratch(micros, width),
            scratch(micros, width),
            scratch(micros, width),
            scratch(micros, width),
            scratch(micros, width),
            scratch(micros, 3 * width),
            pltpu.VMEM((micros, GROUP * pairs, ROW, 2 * ROW), BF16),
            scratch(micros, width),
            scratch(micros, width, F32),
            scratch(micros, width),
            scratch(micros, hid),
            scratch(micros, hid),
            pltpu.VMEM((tokens, width), F32),
            pltpu.VMEM((tokens, width), F32),
            pltpu.VMEM((tokens, width), F32),
            scratch(2, width),
            scratch(2, hid),
            scratch(2, width),
            scratch(2, 3 * width),
            scratch(2, vocab),
            pltpu.VMEM((3, 16, ROW), F32),
            pltpu.VMEM((ROW, ROW), F32),
            pltpu.SemaphoreType.DMA((micros,)),
            pltpu.SemaphoreType.DMA((micros,)),
            pltpu.SemaphoreType.DMA((micros,)),
            pltpu.SemaphoreType.DMA((micros,)),
            pltpu.SemaphoreType.DMA((10, micros)),
        ],
        compiler_params=pltpu.CompilerParams(
            collective_id=0, has_side_effects=True, vmem_limit_bytes=62 * 1024 * 1024
        ),
        name="pipeline",
    )(token_ids, segment_ids, target_ids, *params)


def line_dims(devices):
    dims, stride = [], 1
    if devices == 8:
        return [(2, 1), (4, 2)]
    while devices > 1:
        size = 4 if devices % 4 == 0 else 2
        dims.append((size, stride))
        stride *= size
        devices //= size
    return dims


def chunk_plan(width, hid, vocab, stages, devices):
    slim, deep = width // devices, hid // devices
    plan = [("out", 0, (slim, width), False)]
    for c in range(4):
        plan.append(("down", c, (deep, width // 4), c in (1, 3)))
    for c in range(2):
        plan.append(("extra", c, (stages, vocab // (stages * devices), width // 2), False))
    for c in range(hid // width):
        plan.append(("in", c, (slim, width), c == 1))
    for c in range(3):
        plan.append(("qkv", c, (slim, width), False))
    return plan


def gradient_kernel(stages, devices, plan, *refs):
    dims = line_dims(devices)
    refs = list(refs)

    def take(amount):
        head, refs[:] = refs[:amount], refs[amount:]
        return head

    inputs = take(10)
    vec_in, token_ids = take(2)
    qkv_out, out_out, in_out, down_out, embed_out, head_out, vec_out = take(7)
    local = take(10)
    in_sem = take(1)[0]
    turned_left, turned_xl = take(2)
    mats = dict(
        zip(
            ("normed", "mixed", "normed2", "active", "gres", "ghid", "gbr", "gproj", "xl", "xr"),
            local,
        )
    )
    names = list(mats)
    stage = lax.axis_index("pipe")
    place = lax.axis_index("dp")
    is_extra = (stage == 0) | (stage == stages - 1)
    width = mats["normed"].shape[1]
    where = [lax.rem(place // stride, size) for size, stride in dims]

    barrier = pltpu.get_barrier_semaphore()

    def greet(offset, carry):
        peer = lax.rem(place + offset, devices)
        pl.semaphore_signal(barrier, inc=1, device_id={"dp": peer}, device_id_type=MESH)
        return carry

    def greet_stage(offset, carry):
        peer = lax.rem(stage + offset, stages)
        pl.semaphore_signal(barrier, inc=1, device_id={"pipe": peer}, device_id_type=MESH)
        return carry

    lax.fori_loop(1, devices, greet, 0)
    lax.fori_loop(1, stages, greet_stage, 0)

    def load(name):
        i = names.index(name)
        return pltpu.make_async_copy(inputs[i], mats[name], in_sem.at[i])

    groups = [("mixed", "gbr"), ("gres", "active"), ("xr", "xl"), ("normed2", "ghid"), ("normed", "gproj")]

    def fetch(at):
        if at >= len(groups):
            return
        if groups[at] == ("xr", "xl"):
            @pl.when(is_extra)
            def _():
                load("xr").start()

            @pl.when(stage == stages - 1)
            def _():
                load("xl").start()

            at += 1
        for name in groups[at]:
            load(name).start()

    fetch(0)
    loaded = set()

    def need(*wanted):
        fresh = [name for name in wanted if name not in loaded]
        for name in fresh:
            loaded.add(name)
            load(name).wait()
        if fresh:
            at = [i for i, group in enumerate(groups) if group[0] == fresh[0]][0]
            fetch(at + 1)

    def identity(size):
        here = lax.broadcasted_iota(jnp.int32, (size, size), 0)
        there = lax.broadcasted_iota(jnp.int32, (size, size), 1)
        return jnp.where(here == there, 1.0, 0.0).astype(BF16)

    held = []

    def turn(name):
        if held[-1:] == [name]:
            return
        held.append(name)
        unit = identity(256)
        for q in range(width // 256):
            part = dot_nt(unit, mats[name][:, q * 256 : (q + 1) * 256])
            turned_left[q * 256 : (q + 1) * 256, :] = part.astype(BF16)

    bits = devices.bit_length() - 1
    vec_send, vec_recv = take(2)
    vec_sems = take(2)

    def vec_copy(k):
        peer = jnp.bitwise_xor(place, 1 << k)
        return pltpu.make_async_remote_copy(
            src_ref=vec_send.at[k],
            dst_ref=vec_recv.at[k],
            send_sem=vec_sems[0].at[k],
            recv_sem=vec_sems[1].at[k],
            device_id={"dp": peer},
            device_id_type=MESH,
        )

    def vec_step(k):
        def run():
            if k == 0:
                vec_send[0] = vec_in[...]
                ones = jnp.ones((16, mats["gres"].shape[0]), BF16)
                for name, start, row in (
                    ("gproj", 0, V_QUERY),
                    ("gproj", 2 * width, V_VALUE),
                    ("gbr", 0, V_BRANCH),
                    ("gres", 0, V_RESULT),
                ):
                    part = dot(ones, mats[name][:, start : start + width])
                    vec_send[0, row : row + 1, :] = part[0:1, :]
                for q in range(mats["ghid"].shape[1] // width):
                    part = dot(ones, mats["ghid"][:, q * width : (q + 1) * width])
                    vec_send[0, V_HIDDEN + q : V_HIDDEN + q + 1, :] = part[0:1, :]
            else:
                vec_copy(k - 1).wait_recv()
                vec_send[k] = vec_send[k - 1] + vec_recv[k - 1]
            if k < bits:
                vec_copy(k).start()

        return run

    final_send, final_recv = take(2)
    final_sems = take(2)

    def final_copy(offset):
        peer = lax.rem(stages - 1 + offset, stages)
        return pltpu.make_async_remote_copy(
            src_ref=final_send,
            dst_ref=final_recv,
            send_sem=final_sems[0].at[offset],
            recv_sem=final_sems[1].at[0],
            device_id={"pipe": peer},
            device_id_type=MESH,
        )

    def vec_last():
        vec_step(bits)()
        vec_out[...] = vec_send[bits]

        @pl.when(stage == stages - 1)
        def _():
            final_send[...] = vec_send[bits, 8:16, :]
            for offset in range(1, stages):
                final_copy(offset).start()

    def vec_finish():
        @pl.when(stage != stages - 1)
        def _():
            final_copy(1).wait_recv()
            vec_out[V_FINAL_GAIN : V_FINAL_BIAS + 1, :] = final_recv[
                V_FINAL_GAIN - 8 : V_FINAL_BIAS - 7, :
            ]

    def vec_drain():
        for k in range(bits):
            vec_copy(k).wait_send()

        @pl.when(stage == stages - 1)
        def _():
            for offset in range(1, stages):
                final_copy(offset).wait_send()

    extra_sum, extra_send_sem, extra_recv_sem = take(3)

    def extra_copy(source, offset, target):
        peer = lax.rem(source + offset, stages)
        return pltpu.make_async_remote_copy(
            src_ref=extra_sum.at[peer],
            dst_ref=target,
            send_sem=extra_send_sem.at[offset],
            recv_sem=extra_recv_sem.at[0 if source == 0 else 1],
            device_id={"pipe": peer},
            device_id_type=MESH,
        )

    down_full = {}

    def chunk_steps(kind, c, block, turned):
        order = list(range(len(dims)))
        if turned:
            order.reverse()
        full = take(1)[0]

        def compute():
            if kind == "down":
                need("gres", "active")
                turn("gres")
                if c % 2 == 1:
                    return
                half = width // 2
                lines = slice((c // 2) * half, (c // 2 + 1) * half)
                parts = dot(turned_left[lines, :], mats["active"][...]).astype(BF16)
                depth = block[0]
                unit = identity(depth)
                for d in range(devices):
                    back = dot_nt(unit, parts[:, d * depth : (d + 1) * depth]).astype(BF16)
                    down_full[c][split(d)] = back[:, 0 : half // 2]
                    down_full[c + 1][split(d)] = back[:, half // 2 : half]
            elif kind == "extra":
                vocab = turned_xl.shape[0]
                if c == 0:
                    load("xr").wait()

                @pl.when((stage == 0) & (c == 0))
                def _():
                    rows_n, seq = token_ids.shape
                    places = lax.broadcasted_iota(jnp.int32, (vocab, ROW), 0)
                    gap = jnp.full((1, ROW - seq), -1, jnp.int32)
                    for r in range(rows_n):
                        row = jnp.concatenate([token_ids[r : r + 1, :], gap], axis=1)
                        hot = jnp.where(places == row, 1.0, 0.0)
                        turned_xl[:, r * ROW : (r + 1) * ROW] = hot.astype(BF16)

                @pl.when((stage == stages - 1) & (c == 0))
                def _():
                    load("xl").wait()
                    unit = identity(256)
                    for q in range(vocab // 256):
                        part = dot_nt(unit, mats["xl"][:, q * 256 : (q + 1) * 256])
                        turned_xl[q * 256 : (q + 1) * 256, :] = part.astype(BF16)

                rows = vocab // stages
                for p in range(stages):
                    part = dot(
                        turned_xl[p * rows : (p + 1) * rows, :],
                        mats["xr"][:, c * (width // 2) : (c + 1) * (width // 2)],
                    )
                    part = part.astype(BF16).reshape((devices,) + block[1:])
                    for d in range(devices):
                        full[split(d) + (p,)] = part[d]
            else:
                left, right = {
                    "in": ("normed2", "ghid"),
                    "out": ("mixed", "gbr"),
                    "qkv": ("normed", "gproj"),
                }[kind]
                need(left, right)
                turn(left)
                cols = slice(c * width, (c + 1) * width)
                part = dot(turned_left[...], mats[right][:, cols]).astype(BF16)
                part = part.reshape((devices,) + block)
                for d in range(devices):
                    full[split(d)] = part[d]

        def split(d):
            return tuple((d // stride) % size for size, stride in reversed(dims))

        if kind == "down":
            down_full[c] = full
        steps = [[compute]]
        for at, phase in enumerate(order):
            size = dims[phase][0]
            buffers = take(3)
            done = order[:at]
            last = at == len(order) - 1
            steps[-1].append(functools.partial(line_step, phase, size, 1, full, buffers, done))
            for t in range(2, size):
                steps.append([functools.partial(line_step, phase, size, t, full, buffers, done)])
            drains.append((kind, functools.partial(line_drain, phase, size, full, buffers, done)))
            steps.append([functools.partial(line_final, kind, c, phase, size, full, buffers, done, last)])
        if kind == "extra":
            steps = [[gated([part]) for part in step] for step in steps]
        return steps

    def gated(step):
        def run():
            @pl.when(is_extra)
            def _():
                for part in step:
                    part()

        return run

    def block_of(full, phase, j, done):
        spot = [slice(None)] * len(dims)
        for other in done:
            spot[len(dims) - 1 - other] = where[other]
        spot[len(dims) - 1 - phase] = j
        return full.at[tuple(spot)]

    def line_copy(phase, size, t, side, full, buffers, done):
        recv, ssem, rsem = buffers
        i = where[phase]
        stride = dims[phase][1]
        if side == 0:
            j, peer = size - t + i, place + jnp.where(i < size - 1, stride, 0)
        else:
            j, peer = t - size + i, place - jnp.where(i > 0, stride, 0)
        return pltpu.make_async_remote_copy(
            src_ref=block_of(full, phase, jnp.clip(j, 0, size - 1), done),
            dst_ref=recv.at[0 if size == 2 else side, t - 1],
            send_sem=ssem.at[side, t - 1],
            recv_sem=rsem.at[side, t - 1],
            device_id={"dp": peer},
            device_id_type=MESH,
        )

    def sends(i, size, t, side):
        return (i <= t - 1) if side == 0 else (i >= size - t)

    def line_step(phase, size, t, full, buffers, done):
        i = where[phase]
        for side in range(2):
            at_end = (i == 0) if side == 0 else (i == size - 1)
            j = size - t + i if side == 0 else t - size + i
            j = jnp.clip(j, 0, size - 1)

            @pl.when(sends(i, size, t, side))
            def _():
                if t > 1:
                    @pl.when(jnp.logical_not(at_end))
                    def _():
                        line_copy(phase, size, t - 1, side, full, buffers, done).wait_recv()
                        own = block_of(full, phase, j, done)
                        got = buffers[0][0 if size == 2 else side, t - 2]
                        own[...] = (own[...].astype(F32) + got.astype(F32)).astype(BF16)

                line_copy(phase, size, t, side, full, buffers, done).start()

    def line_final(kind, c, phase, size, full, buffers, done, last):
        i = where[phase]
        own = block_of(full, phase, i, done)
        total = own
        if last:
            slots = {
                "qkv": lambda: qkv_out.at[:, c * width : (c + 1) * width],
                "in": lambda: in_out.at[:, c * width : (c + 1) * width],
                "out": lambda: out_out,
                "down": lambda: down_out.at[:, c * (width // 4) : (c + 1) * (width // 4)],
                "extra": lambda: extra_sum.at[:, :, c * (width // 2) : (c + 1) * (width // 2)],
            }
            total = slots[kind]()
        lower, upper = i > 0, i < size - 1

        def arrived(side):
            line_copy(phase, size, size - 1, side, full, buffers, done).wait_recv()
            return buffers[0][0 if size == 2 else side, size - 2].astype(F32)

        @pl.when(lower & upper)
        def _():
            total[...] = (own[...].astype(F32) + arrived(0) + arrived(1)).astype(total.dtype)

        @pl.when(lower & jnp.logical_not(upper))
        def _():
            total[...] = (own[...].astype(F32) + arrived(0)).astype(total.dtype)

        @pl.when(jnp.logical_not(lower))
        def _():
            total[...] = (own[...].astype(F32) + arrived(1)).astype(total.dtype)

        if last and kind == "extra" and c == 1:
            for source_stage, out in ((0, embed_out), (stages - 1, head_out)):
                @pl.when(stage == source_stage)
                def _():
                    for offset in range(1, stages):
                        extra_copy(source_stage, offset, extra_recv[0 if source_stage == 0 else 1]).start()
                    out[...] = extra_sum[source_stage]

    def line_drain(phase, size, full, buffers, done):
        i = where[phase]
        for side in range(2):
            for t in range(1, size):
                @pl.when(sends(i, size, t, side))
                def _():
                    line_copy(phase, size, t, side, full, buffers, done).wait_send()

    extra_recv = take(2)
    drains = []
    chains = [chunk_steps(*item) for item in plan]
    depth = len(chains[0])
    vec_chain = [vec_step(k) for k in range(bits)] + [vec_last]
    starts, first, extra_rounds = [], 0, iter((1, 3, 6, 8))
    for item in plan:
        if item[3]:
            starts.append(next(extra_rounds))
        else:
            starts.append(first)
            first += 1
    begun = False
    loaded_at = max(start for start, item in zip(starts, plan) if item[0] == "qkv" and item[1] == 0)
    for r in range(max(starts) + depth):
        for d in [0] + list(range(depth - 1, 0, -1)):
            for start, chain in zip(starts, chains):
                if r - start != d:
                    continue
                for part in chain[d]:
                    part()
                    if not begun:
                        begun = True
                        pl.semaphore_wait(barrier, devices - 1 + stages - 1)
        if 0 <= r - loaded_at < len(vec_chain):
            vec_chain[r - loaded_at]()
    vec_finish()
    for source_stage, out in ((0, embed_out), (stages - 1, head_out)):
        @pl.when(stage != source_stage)
        def _():
            got = extra_recv[0 if source_stage == 0 else 1]
            extra_copy(source_stage, 1, got).wait_recv()
            out[...] = got[...]

        @pl.when(stage == source_stage)
        def _():
            for offset in range(1, stages):
                extra_copy(source_stage, offset, extra_recv[0]).wait_send()

    vec_drain()
    for kind, drain in drains:
        if kind == "extra":
            gated([drain])()
        else:
            drain()


def run_gradients(stages, devices, saved, vec, token_ids):
    dims = line_dims(devices)
    rows, tokens, width = saved[0].shape
    hid, vocab = saved[3].shape[2], saved[8].shape[2]
    plan = chunk_plan(width, hid, vocab, stages, devices)
    saved = [member.reshape(rows * tokens, member.shape[2]) for member in saved]
    vmem = pl.BlockSpec(memory_space=pltpu.VMEM)
    hbm = pl.BlockSpec(memory_space=pl.ANY)
    bits = devices.bit_length() - 1
    share = vocab // (stages * devices)
    scratch = [pltpu.VMEM(member.shape, BF16) for member in saved]
    scratch += [pltpu.SemaphoreType.DMA((len(saved),))]
    scratch += [pltpu.VMEM((width, rows * tokens), BF16), pltpu.VMEM((vocab, rows * tokens), BF16)]
    scratch += [
        pltpu.VMEM((bits + 1,) + vec.shape, F32),
        pltpu.VMEM((bits,) + vec.shape, F32),
        pltpu.SemaphoreType.DMA((bits,)),
        pltpu.SemaphoreType.DMA((bits,)),
        pltpu.VMEM((8, width), F32),
        pltpu.VMEM((8, width), F32),
        pltpu.SemaphoreType.DMA((stages,)),
        pltpu.SemaphoreType.DMA((1,)),
        pltpu.VMEM((stages, share, width), F32),
        pltpu.SemaphoreType.DMA((stages,)),
        pltpu.SemaphoreType.DMA((2,)),
        pltpu.VMEM((share, width), F32),
        pltpu.VMEM((share, width), F32),
    ]
    sizes = [size for size, _ in reversed(dims)]
    for _, _, block, turned in plan:
        scratch.append(pltpu.VMEM(tuple(sizes) + block, BF16))
        remain = list(reversed(dims))
        for size, stride in dims[::-1] if turned else dims:
            remain.remove((size, stride))
            piece = tuple(other for other, _ in remain) + block
            scratch.append(pltpu.VMEM((1 if size == 2 else 2, size - 1) + piece, BF16))
            scratch += [pltpu.SemaphoreType.DMA((2, size - 1))] * 2
    return pl.pallas_call(
        functools.partial(gradient_kernel, stages, devices, plan),
        out_shape=[
            jax.ShapeDtypeStruct((width // devices, 3 * width), F32),
            jax.ShapeDtypeStruct((width // devices, width), F32),
            jax.ShapeDtypeStruct((width // devices, hid), F32),
            jax.ShapeDtypeStruct((hid // devices, width), F32),
            jax.ShapeDtypeStruct((share, width), F32),
            jax.ShapeDtypeStruct((share, width), F32),
            jax.ShapeDtypeStruct(vec.shape, F32),
        ],
        in_specs=[hbm] * len(saved) + [vmem] * 2,
        out_specs=[vmem] * 7,
        scratch_shapes=scratch,
        compiler_params=pltpu.CompilerParams(
            collective_id=1, has_side_effects=True, vmem_limit_bytes=62 * 1024 * 1024
        ),
        name="gradients",
    )(*saved, vec, token_ids)


def step_kernel(stages, micros, devices, plan, *refs):
    refs = list(refs)

    def take(amount):
        head, refs[:] = refs[:amount], refs[amount:]
        return head

    token_ids, segment_ids, target_ids = take(3)
    qv_b, out_b, in_b, gains, shifts, fin_gain, fin_bias = take(7)
    embed_h, head_h, qkv_h, out_h, in_h, down_h = take(6)
    qkv_out, out_out, in_out, down_out, embed_out, head_out, vec_out = take(7)
    side, qkv_w, out_w = take(3)
    in_w, down_w = take(4), take(4)
    instream, outb, gin, gs, proj, probs, mixed, middle, active, slope = take(10)
    lo, gmid, s_gbr, s_xl, vec, ids, frames = take(7)
    fsend, frecv, bsend, brecv, wsem = take(5)
    go = lo
    place = lax.axis_index("dp")
    stage = lax.axis_index("pipe")
    tokens, width = instream.shape[1], instream.shape[2]
    hidden_n = in_b.shape[1]
    vocab = side.shape[0]
    pairs = width // ROW
    chunk = 512
    is_first = stage == 0
    is_last = stage == stages - 1
    up = jnp.minimum(stage + 1, stages - 1)
    down = jnp.maximum(stage - 1, 0)

    def bring(index, source, target):
        return pltpu.make_async_copy(source, target, wsem.at[index])

    weights = [bring(1, qkv_h, qkv_w), bring(2, out_h, out_w)]
    for c in range(4):
        lanes = pl.ds(c * chunk, chunk)
        weights.append(bring(3 + c, in_h.at[:, :, :, lanes], in_w[c]))
        weights.append(bring(7 + c, down_h.at[c], down_w[c]))

    @pl.when(is_first)
    def _():
        bring(0, embed_h, side).start()

    for copy in weights:
        copy.start()

    @pl.when(is_last)
    def _():
        bring(0, head_h, side).start()

    barrier = pltpu.get_barrier_semaphore()

    def greet(offset, carry):
        peer = lax.rem(place + offset, devices)
        pl.semaphore_signal(barrier, inc=1, device_id={"dp": peer}, device_id_type=MESH)
        return carry

    def greet_stage(offset, carry):
        peer = lax.rem(stage + offset, stages)
        pl.semaphore_signal(barrier, inc=1, device_id={"pipe": peer}, device_id_type=MESH)
        return carry

    lax.fori_loop(1, devices, greet, 0)
    lax.fori_loop(1, stages, greet_stage, 0)

    def whole(part):
        return part[...].reshape(width, width)

    vec[...] = jnp.zeros_like(vec)
    rows_n, seq = token_ids.shape
    for index, member in enumerate((token_ids, segment_ids, target_ids)):
        ids[index] = jnp.full(ids.shape[1:], 4.0 if index == 1 else -1.0, F32)
        ids[index, 0:rows_n, 0:seq] = member[...].astype(F32)
    at_query = lax.broadcasted_iota(jnp.int32, (ROW, ROW), 1)
    at_key = lax.broadcasted_iota(jnp.int32, (ROW, ROW), 0)
    frames[...] = jnp.where(at_key < ((at_query * 43) // 256) * FRAME + FRAME, 1.0, 0.0)

    def column(index, row):
        values = jnp.broadcast_to(ids[index, pl.ds(row, 1), :], (8, ROW))
        return values.T[:, 0:1]

    def hot_rows(index, m):
        parts = [column(index, m * GROUP + r) for r in range(GROUP)]
        values = jnp.concatenate(parts, axis=0)
        places = lax.broadcasted_iota(jnp.int32, (tokens, vocab), 1).astype(F32)
        return values, jnp.where(values == places, 1.0, 0.0)

    def forward_copy(m):
        return pltpu.make_async_remote_copy(
            src_ref=outb.at[m],
            dst_ref=instream.at[m],
            send_sem=fsend.at[m],
            recv_sem=frecv.at[m],
            device_id={"pipe": up},
            device_id_type=MESH,
        )

    def backward_copy(m):
        return pltpu.make_async_remote_copy(
            src_ref=gs.at[m],
            dst_ref=gin.at[m],
            send_sem=bsend.at[m],
            recv_sem=brecv.at[m],
            device_id={"pipe": down},
            device_id_type=MESH,
        )

    @pl.when(is_first | is_last)
    def _():
        bring(0, embed_h, side).wait()

    for copy in weights:
        copy.wait()
    pl.semaphore_wait(barrier, devices - 1 + stages - 1)

    lane_low = lax.broadcasted_iota(jnp.int32, (ROW, ROW), 1) < ROW // 2

    def forward(m):
        @pl.when(is_first)
        def _():
            hot = hot_rows(0, m)[1].astype(BF16)
            instream[m] = dot(hot, side[...]).astype(BF16)

        @pl.when(jnp.logical_not(is_first))
        def _():
            forward_copy(m).wait_recv()

        normal, _ = normalise(instream[m].astype(F32))
        low = (normal * gains[0:1, :] + shifts[0:1, :]).astype(BF16)
        queries = dot(low, qkv_w[:, 0:width]) + qv_b[0:1, :]
        proj[m, :, 0:width] = (queries * (ROW // 2) ** -0.5).astype(BF16)
        proj[m, :, width : 2 * width] = dot(low, qkv_w[:, width : 2 * width]).astype(BF16)
        proj[m, :, 2 * width : 3 * width] = (
            dot(low, qkv_w[:, 2 * width : 3 * width]) + qv_b[1:2, :]
        ).astype(BF16)
        masks, scores = [], []
        for r in range(GROUP):
            rows = slice(r * ROW, (r + 1) * ROW)
            kinds = lax.broadcasted_iota(jnp.int32, (16, ROW), 0).astype(F32)
            member = jnp.where(ids[1, pl.ds(m * GROUP + r, 1), :] == kinds, 1.0, 0.0).astype(BF16)
            mask = jnp.where(dot_tn(member, member) * frames[...] > 0.5, 0.0, MASKED)
            masks.append(jnp.concatenate([mask, mask], axis=1))
            for p in range(pairs):
                q = stack_pair(proj[m, rows, p * ROW : (p + 1) * ROW], lane_low)
                k = proj[m, rows, width + p * ROW : width + (p + 1) * ROW]
                scores.append(dot_nt(k, q))

        def mix(unit):
            r, p = unit // pairs, unit % pairs
            rows = slice(r * ROW, (r + 1) * ROW)
            v = proj[m, rows, 2 * width + p * ROW : 2 * width + (p + 1) * ROW]
            both = dot_tn(probs[m, unit // 2, unit % 2], v)
            mixed[m, rows, p * ROW : (p + 1) * ROW] = join_pair(both, lane_low).astype(BF16)

        for unit in range(GROUP * pairs):
            masked = scores[unit] + masks[unit // pairs]
            expo = jnp.exp(masked - jnp.max(masked, axis=0, keepdims=True))
            total = jnp.sum(expo, axis=0, keepdims=True)
            probs[m, unit // 2, unit % 2] = (expo * (1.0 / total)).astype(BF16)
            if unit:
                mix(unit - 1)
        mix(GROUP * pairs - 1)
        mid = instream[m].astype(F32) + (dot(mixed[m], out_w[...]) + out_b[0:1, :])
        middle[m] = mid
        normal2, _ = normalise(mid)
        low2 = (normal2 * gains[1:2, :] + shifts[1:2, :]).astype(BF16)
        parts = hidden_n // chunk

        def spread(c):
            return dot(low2, whole(in_w[c]))

        total, ahead = None, spread(0)
        for c in range(parts):
            cols = slice(c * chunk, (c + 1) * chunk)
            hid = ahead + in_b[0:1, cols]
            if c + 1 < parts:
                ahead = spread(c + 1)
            square = hid * hid
            tan = jnp.tanh(hid * (GELU_A + (GELU_A * GELU_B) * square))
            half = 0.5 + 0.5 * tan
            act = (hid * half).astype(BF16)
            active[m, :, cols] = act
            rise = (1.0 - tan * tan) * (0.5 * GELU_A + (1.5 * GELU_A * GELU_B) * square)
            slope[m, :, cols] = (half + hid * rise).astype(BF16)
            term = dot(act, whole(down_w[c]))
            total = term if total is None else total + term
        lo[...] = middle[m] + (total + out_b[1:2, :])

        @pl.when(jnp.logical_not(is_last))
        def _():
            outb[m] = lo[...].astype(BF16)
            forward_copy(m).start()

    def head(m):
        normal, scale = normalise(lo[...])
        outb[m] = (normal * fin_gain[...] + fin_bias[...]).astype(BF16)
        logits = dot_nt(outb[m], side[...])
        top = jnp.max(logits, axis=-1, keepdims=True)
        expo = jnp.exp(logits - top)
        total = jnp.sum(expo, axis=-1, keepdims=True)
        target, hot = hot_rows(2, m)
        grad_logits = jnp.where(target >= 0.0, expo * (1.0 / total) - hot, 0.0).astype(BF16)
        s_xl[m] = grad_logits
        grad_final = dot(grad_logits, side[...])
        vec[V_FINAL_GAIN : V_FINAL_GAIN + 1, :] += column_sum(grad_final * normal)
        vec[V_FINAL_BIAS : V_FINAL_BIAS + 1, :] += column_sum(grad_final)
        go[...] = norm_backward(grad_final, normal, scale, fin_gain[...])

    def backward(m):
        @pl.when(jnp.logical_not(is_last))
        def _():
            backward_copy(m).wait_recv()
            go[...] = gin[m].astype(F32)

        gres = go[...].astype(BF16)
        gin[m] = gres
        parts = hidden_n // chunk

        def spread(c):
            return dot_nt(gres, whole(down_w[c]))

        total, ahead = None, spread(0)
        for c in range(parts):
            cols = slice(c * chunk, (c + 1) * chunk)
            gact = ahead
            if c + 1 < parts:
                ahead = spread(c + 1)
            ghid = (gact * slope[m, :, cols].astype(F32)).astype(BF16)
            slope[m, :, cols] = ghid
            term = dot_nt(ghid, whole(in_w[c]))
            total = term if total is None else total + term
        normal2, scale2 = normalise(middle[m])
        vec[V_GAIN2 : V_GAIN2 + 1, :] += column_sum(total * normal2)
        vec[V_SHIFT2 : V_SHIFT2 + 1, :] += column_sum(total)
        gmid[...] = go[...] + norm_backward(total, normal2, scale2, gains[1:2, :])
        gbr = gmid[...].astype(BF16)
        s_gbr[m] = gbr
        gmix = dot_nt(gbr, out_w[...]).astype(BF16)
        grads = []
        for r in range(GROUP):
            rows = slice(r * ROW, (r + 1) * ROW)
            for p in range(pairs):
                gm = stack_pair(gmix[rows, p * ROW : (p + 1) * ROW], lane_low)
                vlanes = slice(2 * width + p * ROW, 2 * width + (p + 1) * ROW)
                grads.append(dot_nt(proj[m, rows, vlanes], gm))
                unit = r * pairs + p
                proj[m, rows, vlanes] = dot(probs[m, unit // 2, unit % 2], gm).astype(BF16)

        def pull(unit, gsc):
            r, p = unit // pairs, unit % pairs
            rows = slice(r * ROW, (r + 1) * ROW)
            lanes = slice(p * ROW, (p + 1) * ROW)
            klanes = slice(width + p * ROW, width + (p + 1) * ROW)
            q = stack_pair(proj[m, rows, lanes], lane_low)
            gq = join_pair(dot_tn(gsc, proj[m, rows, klanes]), lane_low) * (ROW // 2) ** -0.5
            gk = dot(gsc, q)
            proj[m, rows, klanes] = gk.astype(BF16)
            proj[m, rows, lanes] = gq.astype(BF16)

        waiting = None
        for unit in range(GROUP * pairs):
            weights = probs[m, unit // 2, unit % 2].astype(F32)
            inner = jnp.sum(weights * grads[unit], axis=0, keepdims=True)
            gsc = (weights * (grads[unit] - inner)).astype(BF16)
            if waiting is not None:
                pull(unit - 1, waiting)
            waiting = gsc
        pull(GROUP * pairs - 1, waiting)
        gproj = proj[m]
        gnormed = dot_nt(gproj, qkv_w[...])
        normal, scale = normalise(instream[m].astype(F32))
        vec[V_GAIN1 : V_GAIN1 + 1, :] += column_sum(gnormed * normal)
        vec[V_SHIFT1 : V_SHIFT1 + 1, :] += column_sum(gnormed)
        gs[m] = (gmid[...] + norm_backward(gnormed, normal, scale, gains[0:1, :])).astype(BF16)

        @pl.when(jnp.logical_not(is_first))
        def _():
            backward_copy(m).start()

    def tick(t, carry):
        m_forward = t - stage
        m_backward = t - (2 * (stages - 1) - stage)

        @pl.when((m_forward >= 0) & (m_forward < micros))
        def _():
            forward(m_forward)

        @pl.when((m_backward >= 0) & (m_backward < micros))
        def _():
            @pl.when(is_last)
            def _():
                head(m_backward)

            backward(m_backward)

        return carry

    lax.fori_loop(0, micros + 2 * (stages - 1), tick, 0)

    embed_stage = stages - 2
    is_extra = (stage == embed_stage) | is_last
    dims = line_dims(devices)
    turned_left = qkv_w
    mats = {
        "mixed": mixed,
        "active": active,
        "gres": gin,
        "ghid": slope,
        "gbr": s_gbr,
        "gproj": proj,
    }

    def mat(name, lanes=slice(None)):
        value = mats[name][:, :, lanes]
        return value.reshape(micros * tokens, value.shape[2])

    where = [lax.rem(place // stride, size) for size, stride in dims]

    def identity(size):
        here = lax.broadcasted_iota(jnp.int32, (size, size), 0)
        there = lax.broadcasted_iota(jnp.int32, (size, size), 1)
        return jnp.where(here == there, 1.0, 0.0).astype(BF16)

    held = []

    def turn(name):
        if held[-1:] == [name]:
            return
        held.append(name)
        unit = identity(256)
        if name in ("normed", "normed2"):
            row = 0 if name == "normed" else 1
            source = instream if name == "normed" else middle
            for m in range(micros):
                normal, _ = normalise(source[m].astype(F32))
                again = (normal * gains[row : row + 1, :] + shifts[row : row + 1, :]).astype(BF16)
                for q in range(width // 256):
                    part = dot_nt(unit, again[:, q * 256 : (q + 1) * 256])
                    turned_left[q * 256 : (q + 1) * 256, m * tokens : (m + 1) * tokens] = part.astype(BF16)
            return
        for q in range(width // 256):
            part = dot_nt(unit, mat(name, slice(q * 256, (q + 1) * 256)))
            turned_left[q * 256 : (q + 1) * 256, :] = part.astype(BF16)

    bits = devices.bit_length() - 1
    vec_send, vec_recv = take(2)
    vec_sems = take(2)

    def vec_copy(k):
        peer = jnp.bitwise_xor(place, 1 << k)
        return pltpu.make_async_remote_copy(
            src_ref=vec_send.at[k],
            dst_ref=vec_recv.at[k],
            send_sem=vec_sems[0].at[k],
            recv_sem=vec_sems[1].at[k],
            device_id={"dp": peer},
            device_id_type=MESH,
        )

    def vec_step(k):
        def run():
            if k == 0:
                vec_send[0] = vec[...]
                ones = jnp.ones((16, micros * tokens), BF16)
                for name, start, row in (
                    ("gproj", 0, V_QUERY),
                    ("gproj", 2 * width, V_VALUE),
                    ("gbr", 0, V_BRANCH),
                    ("gres", 0, V_RESULT),
                ):
                    part = dot(ones, mat(name, slice(start, start + width)))
                    vec_send[0, row : row + 1, :] = part[0:1, :]
                for q in range(hidden_n // width):
                    part = dot(ones, mat("ghid", slice(q * width, (q + 1) * width)))
                    vec_send[0, V_HIDDEN + q : V_HIDDEN + q + 1, :] = part[0:1, :]
            else:
                vec_copy(k - 1).wait_recv()
                vec_send[k] = vec_send[k - 1] + vec_recv[k - 1]
            if k < bits:
                vec_copy(k).start()

        return run

    final_send, final_recv = take(2)
    final_sems = take(2)

    def final_copy(offset):
        peer = lax.rem(stages - 1 + offset, stages)
        return pltpu.make_async_remote_copy(
            src_ref=final_send,
            dst_ref=final_recv,
            send_sem=final_sems[0].at[offset],
            recv_sem=final_sems[1].at[0],
            device_id={"pipe": peer},
            device_id_type=MESH,
        )

    def vec_last():
        vec_step(bits)()
        vec_out[...] = vec_send[bits]

        @pl.when(stage == stages - 1)
        def _():
            final_send[...] = vec_send[bits, 8:16, :]
            for offset in range(1, stages):
                final_copy(offset).start()

    def vec_finish():
        @pl.when(stage != stages - 1)
        def _():
            final_copy(1).wait_recv()
            vec_out[V_FINAL_GAIN : V_FINAL_BIAS + 1, :] = final_recv[
                V_FINAL_GAIN - 8 : V_FINAL_BIAS - 7, :
            ]

    def vec_drain():
        for k in range(bits):
            vec_copy(k).wait_send()

        @pl.when(stage == stages - 1)
        def _():
            for offset in range(1, stages):
                final_copy(offset).wait_send()

    def ship():
        return pltpu.make_async_remote_copy(
            src_ref=s_xl.at[pl.ds(0, 2)],
            dst_ref=s_xl.at[pl.ds(0, 2)],
            send_sem=ship_sem.at[0],
            recv_sem=ship_sem.at[1],
            device_id={"pipe": embed_stage},
            device_id_type=MESH,
        )

    def ship_embed():
        rows, half = vocab // stages, width // 2

        @pl.when(is_first)
        def _():
            right = gs[...].reshape(micros * tokens, width)
            for p in range(stages):
                here = lax.broadcasted_iota(jnp.int32, (rows, ROW), 0).astype(F32) + p * rows
                hot = [
                    jnp.where(ids[0, r : r + 1, :] == here, 1.0, 0.0).astype(BF16) for r in range(rows_n)
                ]
                part = dot(jnp.concatenate(hot, axis=1), right).astype(BF16)
                for k in range(2):
                    s_xl[k, :, p * half : (p + 1) * half] = part[:, k * half : (k + 1) * half]
            ship().start()

    extra_sum, extra_send_sem, extra_recv_sem, last_sum, ship_sem = take(5)
    share = embed_out.shape[0]

    def extra_copy(source, offset, target):
        peer = lax.rem(source + offset, stages)
        return pltpu.make_async_remote_copy(
            src_ref=extra_sum.at[pl.ds(pl.multiple_of(peer * share, share), share)],
            dst_ref=target,
            send_sem=extra_send_sem.at[offset],
            recv_sem=extra_recv_sem.at[0 if source == embed_stage else 1],
            device_id={"pipe": peer},
            device_id_type=MESH,
        )

    def chunk_steps(kind, c, block, turned):
        order = list(range(len(dims)))
        if turned:
            order.reverse()
        if kind == "down":
            full = probs.at[c]
        elif kind == "extra":
            full = probs.at[4 + c]
        else:
            full = (down_w + in_w)[{"out": 0, "in": 1, "qkv": 5}[kind] + c]

        def compute():
            if kind == "down":
                if c % 2 == 1:
                    return
                turn("gres")
                half = width // 2
                lines = slice((c // 2) * half, (c // 2 + 1) * half)
                parts = dot(turned_left[lines, :], mat("active")).astype(BF16)
                depth = hidden_n // devices
                unit = identity(depth)
                for d in range(devices):
                    back = dot_nt(unit, parts[:, d * depth : (d + 1) * depth]).astype(BF16)
                    for k in range(2):
                        piece = back[:, k * ROW : (k + 1) * ROW]
                        piece = jnp.concatenate([piece[: depth // 2], piece[depth // 2 :]], axis=1)
                        probs[(c + k,) + split(d)] = piece
            elif kind == "extra":
                if c == 1:
                    return
                rows = vocab // stages
                share = rows // devices
                half = width // 2

                def fill(left, right):
                    for p in range(stages):
                        part = left(p, right).astype(BF16).reshape(devices, share, width)
                        for d in range(devices):
                            for k in range(2):
                                lines = slice(p * share, (p + 1) * share)
                                probs[(4 + k,) + split(d) + (lines,)] = part[
                                    d, :, k * half : (k + 1) * half
                                ]

                def flat(ref):
                    return ref[...].reshape(micros * tokens, ref.shape[2])

                @pl.when(stage == embed_stage)
                def _():
                    ship().wait_recv()
                    for d in range(devices):
                        for k in range(2):
                            for p in range(stages):
                                lines = slice(p * share, (p + 1) * share)
                                probs[(4 + k,) + split(d) + (lines,)] = s_xl[
                                    k, d * share : (d + 1) * share, p * half : (p + 1) * half
                                ]

                @pl.when(is_last)
                def _():
                    def soft_part(p, right):
                        left = s_xl[:, :, p * rows : (p + 1) * rows]
                        return dot_tn(left.reshape(micros * tokens, rows), right)

                    fill(soft_part, flat(outb))
            else:
                left, right = {
                    "in": ("normed2", "ghid"),
                    "out": ("mixed", "gbr"),
                    "qkv": ("normed", "gproj"),
                }[kind]
                turn(left)
                part = dot(turned_left[...], mat(right, slice(c * width, (c + 1) * width)))
                part = part.astype(BF16).reshape((devices,) + block)
                for d in range(devices):
                    full[split(d)] = part[d]

        def split(d):
            return tuple((d // stride) % size for size, stride in reversed(dims))

        steps = [[compute]]
        for at, phase in enumerate(order):
            size = dims[phase][0]
            buffers = take(3)
            done = order[:at]
            last = at == len(order) - 1
            steps[-1].append(functools.partial(line_step, phase, size, 1, full, buffers, done))
            for t in range(2, size):
                steps.append([functools.partial(line_step, phase, size, t, full, buffers, done)])
            drains.append((kind, functools.partial(line_drain, phase, size, full, buffers, done)))
            steps.append([functools.partial(line_final, kind, c, phase, size, full, buffers, done, last)])
        if kind == "extra":
            steps = [[gated([part]) for part in step] for step in steps]
        return steps

    def gated(step):
        def run():
            @pl.when(is_extra)
            def _():
                for part in step:
                    part()

        return run

    def block_of(full, phase, j, done):
        spot = [slice(None)] * len(dims)
        for other in done:
            spot[len(dims) - 1 - other] = where[other]
        spot[len(dims) - 1 - phase] = j
        return full.at[tuple(spot)]

    def line_copy(phase, size, t, side, full, buffers, done):
        recv, ssem, rsem = buffers
        i = where[phase]
        stride = dims[phase][1]
        if side == 0:
            j, peer = size - t + i, place + jnp.where(i < size - 1, stride, 0)
        else:
            j, peer = t - size + i, place - jnp.where(i > 0, stride, 0)
        return pltpu.make_async_remote_copy(
            src_ref=block_of(full, phase, jnp.clip(j, 0, size - 1), done),
            dst_ref=recv.at[0 if size == 2 else side, t - 1],
            send_sem=ssem.at[side, t - 1],
            recv_sem=rsem.at[side, t - 1],
            device_id={"dp": peer},
            device_id_type=MESH,
        )

    def sends(i, size, t, side):
        return (i <= t - 1) if side == 0 else (i >= size - t)

    def line_step(phase, size, t, full, buffers, done):
        i = where[phase]
        for side in range(2):
            at_end = (i == 0) if side == 0 else (i == size - 1)
            j = size - t + i if side == 0 else t - size + i
            j = jnp.clip(j, 0, size - 1)

            @pl.when(sends(i, size, t, side))
            def _():
                if t > 1:
                    @pl.when(jnp.logical_not(at_end))
                    def _():
                        line_copy(phase, size, t - 1, side, full, buffers, done).wait_recv()
                        own = block_of(full, phase, j, done)
                        got = buffers[0][0 if size == 2 else side, t - 2]
                        own[...] = (own[...].astype(F32) + got.astype(F32)).astype(BF16)

                line_copy(phase, size, t, side, full, buffers, done).start()

    def line_final(kind, c, phase, size, full, buffers, done, last):
        i = where[phase]
        own = block_of(full, phase, i, done)
        total = own
        if last:
            lanes = slice(c * width, (c + 1) * width)
            slots = {
                "qkv": lambda: qkv_out.at[:, lanes],
                "in": lambda: in_out.at[:, lanes],
                "out": lambda: out_out,
                "down": lambda: last_sum,
                "extra": lambda: extra_sum.at[:, c * (width // 2) : (c + 1) * (width // 2)],
            }
            total = slots[kind]()
        lower, upper = i > 0, i < size - 1

        def arrived(side):
            line_copy(phase, size, size - 1, side, full, buffers, done).wait_recv()
            return buffers[0][0 if size == 2 else side, size - 2].astype(F32)

        @pl.when(lower & upper)
        def _():
            total[...] = (own[...].astype(F32) + arrived(0) + arrived(1)).astype(total.dtype)

        @pl.when(lower & jnp.logical_not(upper))
        def _():
            total[...] = (own[...].astype(F32) + arrived(0)).astype(total.dtype)

        @pl.when(jnp.logical_not(lower))
        def _():
            total[...] = (own[...].astype(F32) + arrived(1)).astype(total.dtype)

        if last and kind == "down":
            deep = down_out.shape[0] // 2
            lanes = slice(c * ROW, (c + 1) * ROW)
            down_out[0:deep, lanes] = last_sum[:, 0:ROW]
            down_out[deep : 2 * deep, lanes] = last_sum[:, ROW : 2 * ROW]
        if last and kind == "extra" and c == 1:
            for source_stage, out in ((embed_stage, embed_out), (stages - 1, head_out)):
                @pl.when(stage == source_stage)
                def _():
                    for offset in range(1, stages):
                        extra_copy(source_stage, offset, extra_recv[0 if source_stage == embed_stage else 1]).start()
                    out[...] = extra_sum[source_stage * share : (source_stage + 1) * share, :]

    def line_drain(phase, size, full, buffers, done):
        i = where[phase]
        for side in range(2):
            for t in range(1, size):
                @pl.when(sends(i, size, t, side))
                def _():
                    line_copy(phase, size, t, side, full, buffers, done).wait_send()

    extra_recv = take(2)
    drains = []
    chains = [chunk_steps(*item) for item in plan]
    depth = len(chains[0])
    vec_chain = [vec_step(k) for k in range(bits)] + [vec_last]
    starts, first, extra_rounds = [], 0, iter((1, 3, 5, 7))
    for item in plan:
        if item[0] == "extra":
            starts.append(7 + item[1])
        elif item[3]:
            starts.append(next(extra_rounds))
        else:
            starts.append(first)
            first += 1
    loaded_at = max(start for start, item in zip(starts, plan) if item[0] == "qkv" and item[1] == 0)
    for r in range(max(starts) + depth):
        for d in [0] + list(range(depth - 1, 0, -1)):
            for start, chain in zip(starts, chains):
                if r - start != d:
                    continue
                for part in chain[d]:
                    part()
            if r == 1 and d == 0:
                ship_embed()
        if 0 <= r - loaded_at < len(vec_chain):
            vec_chain[r - loaded_at]()
    vec_finish()
    for source_stage, out in ((embed_stage, embed_out), (stages - 1, head_out)):
        @pl.when(stage != source_stage)
        def _():
            got = extra_recv[0 if source_stage == embed_stage else 1]
            extra_copy(source_stage, 1, got).wait_recv()
            out[...] = got[...]

        @pl.when(stage == source_stage)
        def _():
            for offset in range(1, stages):
                extra_copy(source_stage, offset, extra_recv[0]).wait_send()

    vec_drain()
    for kind, drain in drains:
        if kind == "extra":
            gated([drain])()
        else:
            drain()

    @pl.when(is_first)
    def _():
        ship().wait_send()

    for m in range(micros):
        @pl.when(jnp.logical_not(is_last))
        def _():
            forward_copy(m).wait_send()

        @pl.when(jnp.logical_not(is_first))
        def _():
            backward_copy(m).wait_send()


def step_plan(width, hid, vocab, stages, devices):
    plan = []
    for kind, c, _, turned in chunk_plan(width, hid, vocab, stages, devices):
        wide = kind in ("down", "extra")
        plan.append((kind, c, (ROW, 2 * ROW) if wide else (width // devices, width), turned))
    extra = [item for item in plan if item[0] == "extra"]
    rest = [item for item in plan if item[0] != "extra"]
    return rest + extra


def run_step(stages, devices, token_ids, segment_ids, target_ids, params):
    embed, qkv_w, qv_b, out_w, out_b, in_w, in_b, down_w, gains, shifts, fg, fb, head_w = params
    dims = line_dims(devices)
    width, hid, vocab = embed.shape[1], in_w.shape[1], head_w.shape[0]
    tokens = GROUP * ROW
    micros = token_ids.shape[0] // GROUP
    vmem = pl.BlockSpec(memory_space=pltpu.VMEM)
    hbm = pl.BlockSpec(memory_space=pl.ANY)
    sizes = tuple(size for size, _ in reversed(dims))
    slim = width // devices
    share = vocab // (stages * devices)
    plan = step_plan(width, hid, vocab, stages, devices)
    bits = devices.bit_length() - 1

    def scratch(lead, columns, kind=BF16):
        return pltpu.VMEM((lead, tokens, columns), kind)

    def sums(*shape):
        return pltpu.VMEM(shape, F32)

    dma = pltpu.SemaphoreType.DMA
    scratch_shapes = [
        pltpu.VMEM((vocab, width), BF16),
        pltpu.VMEM((width, 3 * width), BF16),
        pltpu.VMEM((width, width), BF16),
    ]
    scratch_shapes += [pltpu.VMEM(sizes + (slim, width), BF16)] * 8
    scratch_shapes += [
        scratch(micros, width),
        scratch(micros, width),
        scratch(micros, width),
        scratch(micros, width),
        scratch(micros, 3 * width),
        pltpu.VMEM((micros,) + sizes + (ROW, 2 * ROW), BF16),
        scratch(micros, width),
        scratch(micros, width, F32),
        scratch(micros, hid),
        scratch(micros, hid),
        sums(tokens, width),
        sums(tokens, width),
        scratch(micros, width),
        scratch(micros, vocab),
        sums(VEC_ROWS, width),
        sums(3, 16, ROW),
        sums(ROW, ROW),
        dma((micros,)),
        dma((micros,)),
        dma((micros,)),
        dma((micros,)),
        dma((11,)),
        sums(bits + 1, VEC_ROWS, width),
        sums(bits, VEC_ROWS, width),
        dma((bits,)),
        dma((bits,)),
        sums(8, width),
        sums(8, width),
        dma((stages,)),
        dma((1,)),
        sums(stages * share, width),
        dma((stages,)),
        dma((2,)),
        sums(ROW, 2 * ROW),
        dma((2,)),
        sums(share, width),
        sums(share, width),
    ]
    for _, _, block, turned in plan:
        remain = list(reversed(dims))
        for size, stride in dims[::-1] if turned else dims:
            remain.remove((size, stride))
            piece = tuple(other for other, _ in remain) + block
            scratch_shapes.append(pltpu.VMEM((1 if size == 2 else 2, size - 1) + piece, BF16))
            scratch_shapes += [dma((2, size - 1))] * 2

    def result(*shape):
        return jax.ShapeDtypeStruct(shape, F32)

    return pl.pallas_call(
        functools.partial(step_kernel, stages, micros, devices, plan),
        out_shape=[
            result(slim, 3 * width),
            result(slim, width),
            result(slim, hid),
            result(hid // devices, width),
            result(share, width),
            result(share, width),
            result(VEC_ROWS, width),
        ],
        in_specs=[vmem] * 10 + [hbm] * 6,
        out_specs=[vmem] * 7,
        scratch_shapes=scratch_shapes,
        compiler_params=pltpu.CompilerParams(
            collective_id=2, has_side_effects=True, vmem_limit_bytes=63 * 1024 * 1024
        ),
        name="step",
    )(
        token_ids,
        segment_ids,
        target_ids,
        qv_b,
        out_b,
        in_b,
        gains,
        shifts,
        fg,
        fb,
        embed,
        head_w,
        qkv_w,
        out_w,
        in_w.reshape(sizes + (slim, hid)),
        down_w.reshape((hid // width,) + sizes + (slim, width)),
    )


def finish_kernel(devices, embed_g, qkv_g, out_g, in_g, down_g, head_g, vec, *outs):
    place = lax.axis_index("dp")
    width = vec.shape[1]
    (embed_o, qkv_o, qv_o, out_o, outb_o, in_o, inb_o, down_o, gain_o, shift_o, fg_o, fb_o, head_o) = outs
    embed_o[...] = embed_g[...]
    head_o[...] = head_g[...]
    for source, target in ((qkv_g, qkv_o), (out_g, out_o), (in_g, in_o), (down_g, down_o)):
        target[0] = source[...]
    lanes = width // devices
    turned = pltpu.roll(vec[0:8, :], lax.rem(width - place * lanes, width), 1)
    for row, out in ((V_QUERY, qv_o), (V_BRANCH, outb_o), (V_GAIN1, gain_o), (V_SHIFT1, shift_o)):
        out[0] = turned[row : row + 2, 0:lanes]
    share = inb_o.shape[1]
    first = place * share
    row = vec[pl.ds(V_HIDDEN + first // width, 1), :]
    wide = jnp.broadcast_to(row, (8, width))
    inb_o[...] = pltpu.roll(wide, lax.rem(width - lax.rem(first, width), width), 1)[0:1, 0:share]
    fg_o[...] = vec[V_FINAL_GAIN : V_FINAL_GAIN + 1, :]
    fb_o[...] = vec[V_FINAL_BIAS : V_FINAL_BIAS + 1, :]


def run_finish(devices, embed_g, qkv_g, out_g, in_g, down_g, head_g, vec):
    vmem = pl.BlockSpec(memory_space=pltpu.VMEM)
    width = vec.shape[1]
    lanes = width // devices

    def shape(*sizes):
        return jax.ShapeDtypeStruct(sizes, F32)

    pair = shape(1, 2, lanes)
    return pl.pallas_call(
        functools.partial(finish_kernel, devices),
        out_shape=[
            shape(*embed_g.shape),
            shape(1, *qkv_g.shape),
            pair,
            shape(1, *out_g.shape),
            pair,
            shape(1, *in_g.shape),
            shape(1, in_g.shape[1] // devices),
            shape(1, *down_g.shape),
            pair,
            pair,
            shape(1, width),
            shape(1, width),
            shape(*head_g.shape),
        ],
        in_specs=[vmem] * 7,
        out_specs=[vmem] * 13,
        name="finish",
    )(embed_g, qkv_g, out_g, in_g, down_g, head_g, vec)


def on_device(
    token_ids,
    segment_ids,
    target_ids,
    embed_table,
    qkv_weight,
    qv_bias,
    out_weight,
    out_biases,
    ff_in,
    ff_in_bias,
    ff_out,
    norm_gains,
    norm_biases,
    final_gain,
    final_bias,
    head_weight,
):
    stages = lax.axis_size("pipe")
    devices = lax.axis_size("dp")
    params = (
        embed_table,
        qkv_weight[0],
        qv_bias[0],
        out_weight[0],
        out_biases[0],
        ff_in[0],
        ff_in_bias,
        ff_out[0],
        norm_gains[0],
        norm_biases[0],
        final_gain[None],
        final_bias[None],
        head_weight,
    )
    if devices == 8:
        grads = run_step(stages, devices, token_ids, segment_ids, target_ids, params)
    else:
        *saved, vec = run_pipeline(stages, token_ids, segment_ids, target_ids, params)
        grads = run_gradients(stages, devices, saved, vec, token_ids)
    qkv_g, out_g, in_g, down_g, embed_g, head_g, sums = grads
    done = list(run_finish(devices, embed_g, qkv_g, out_g, in_g, down_g, head_g, sums))
    done[10], done[11] = done[10][0], done[11][0]
    return tuple(done)


def solution(mesh):
    layer3 = P("pipe", None, None)
    return jax.shard_map(
        on_device,
        mesh=mesh,
        in_specs=(
            P("dp", None),
            P("dp", None),
            P("dp", None),
            P(),
            layer3,
            layer3,
            layer3,
            layer3,
            layer3,
            P("pipe", None),
            layer3,
            layer3,
            layer3,
            P(),
            P(),
            P(),
        ),
        out_specs=(
            P(("pipe", "dp"), None),
            P("pipe", "dp", None),
            P("pipe", None, "dp"),
            P("pipe", "dp", None),
            P("pipe", None, "dp"),
            P("pipe", "dp", None),
            P("pipe", "dp"),
            P("pipe", "dp", None),
            P("pipe", None, "dp"),
            P("pipe", None, "dp"),
            P(),
            P(),
            P(("pipe", "dp"), None),
        ),
        check_vma=False,
    )
```

profile of v0, /device:TPU:0, one launch (start us, length us, event | category | flops | bytes accessed | tf_op | source)
XLA Modules:
  0.0 176.9 jit_solution(15496448183133170206)
XLA Ops:
  0.7 173.4 %step.1 = (f32[64,1536]{1,0:T(8,128)}, f32[64,512]{1,0:T(8,128)}, f32[64,2048]{1,0:T(8,128)}, f32[256,512]{1,0:T(8,128)}, f32[32,512]{1,0:T(8,128)}, /*index=5*/f32[32,512]{1,0:T(8,128)}, f32[16,512]{1,0:T(8,128)}) custom-call(s32[12,126]{1,0:T(8,128)} %refs_0_.1, s32[12,126]{1,0:T(8,128)} %refs_1_.1, s32[12,126]{1,0:T(8,128)} %refs_2_.1, ...), custom_call_target="tpu_custom_call" | custom-call | tf_op jit(solution)/shard_map/step/pallas_call | solution.py:1840
  174.1 2.6 %finish.1 = (f32[32,512]{1,0:T(8,128)}, f32[1,64,1536]{2,1,0:T(8,128)}, f32[1,2,64]{2,1,0:T(2,128)}, f32[1,64,512]{2,1,0:T(8,128)}, f32[1,2,64]{2,1,0:T(2,128)},...) custom-call(f32[32,512]{1,0:T(8,128)} %get-tuple-element.33.embed_g,, ...), custom_call_target="tpu_custom_call" | custom-call | tf_op jit(solution)/shard_map/finish/pallas_call | solution.py:1908
where the time goes:
time: 177 us
  Pallas kernels  176 us (99%)
    pallas_call x1, Pallas kernels, run_step(): pl.pallas_call(functools.partial(step_kernel, stages, micros, devices, pl...  173 us

commit v1 on v0

--- a/solution.py
+++ b/solution.py
@@ -1695,7 +1695,7 @@
     chains = [chunk_steps(*item) for item in plan]
     depth = len(chains[0])
     vec_chain = [vec_step(k) for k in range(bits)] + [vec_last]
-    starts, first, extra_rounds = [], 0, iter((1, 3, 5, 7))
+    starts, first, extra_rounds = [], 0, iter((1, 2, 4, 6))
     for item in plan:
         if item[0] == "extra":
             starts.append(7 + item[1])

time: 177 us -> 176 us (level)
  no operation moved by 1% of the time
where the time goes in v1:
time: 176 us
  Pallas kernels  175 us (99%)
    pallas_call x1, Pallas kernels, run_step(): pl.pallas_call(functools.partial(step_kernel, stages, micros, devices, pl...  172 us

profile of v1, /device:TPU:0, one launch (start us, length us, event | category | flops | bytes accessed | tf_op | source)
XLA Modules:
  0.0 175.9 jit_solution(7263838436284676813)
XLA Ops:
  0.7 172.5 %step.1 = (f32[64,1536]{1,0:T(8,128)}, f32[64,512]{1,0:T(8,128)}, f32[64,2048]{1,0:T(8,128)}, f32[256,512]{1,0:T(8,128)}, f32[32,512]{1,0:T(8,128)}, /*index=5*/f32[32,512]{1,0:T(8,128)}, f32[16,512]{1,0:T(8,128)}) custom-call(s32[12,126]{1,0:T(8,128)} %refs_0_.1, s32[12,126]{1,0:T(8,128)} %refs_1_.1, s32[12,126]{1,0:T(8,128)} %refs_2_.1, ...), custom_call_target="tpu_custom_call" | custom-call | tf_op jit(solution)/shard_map/step/pallas_call | solution.py:1840
  173.1 2.6 %finish.1 = (f32[32,512]{1,0:T(8,128)}, f32[1,64,1536]{2,1,0:T(8,128)}, f32[1,2,64]{2,1,0:T(2,128)}, f32[1,64,512]{2,1,0:T(8,128)}, f32[1,2,64]{2,1,0:T(2,128)},...) custom-call(f32[32,512]{1,0:T(8,128)} %get-tuple-element.33.embed_g,, ...), custom_call_target="tpu_custom_call" | custom-call | tf_op jit(solution)/shard_map/finish/pallas_call | solution.py:1908
